TPU v7x, 32 devices: a whole 2x2x4 slice. The times are simulated.
32 devices in a mesh: arch: 2 (over core), dom: 16 (over z, y, x).
Axes of the slice: x: 2, y: 2, z: 4, core: 2. Of those that a mesh axis runs over, the one named last changes fastest.
Arguments:
- position: float32 [3, 131072], P(None, ('arch', 'dom')), may hold values from -6 to 6
- particle_mass: float32 [131072], P(('arch', 'dom')), may hold values from 0.5 to 2
- settling: float32 [131072], P(('arch', 'dom')), may hold values from 0.05 to 1
- walk_noise: float32 [3, 3, 131072], P(None, None, ('arch', 'dom')), may hold values from -6 to 6
- velocity: bfloat16 [4, 3, 32, 2048], P(None, None, ('arch', 'dom')), may hold values from -6 to 6
- diffusivity: bfloat16 [4, 32, 2048], P(None, ('arch', 'dom')), may hold values from 0.019897461 to 0.5
- block_tile: int32 [3, 32, 16], P(None, ('arch', 'dom')), may hold values from 0 to 31, as said below
- cell_index: int32 [3, 131072], P(None, ('arch', 'dom')), may hold values from 0 to 2047
- bed_cell: int32 [3, 131072], P(None, ('arch', 'dom')), may hold values from 0 to 511
- route_code: int32 [2, 32, 16], P(None, ('arch', 'dom')), may hold values from 0 to 15, each once within a row
Outputs:
- final_position: float32 [3, 131072], P(None, ('arch', 'dom'))
- final_mass: float32 [131072], P(('arch', 'dom'))
- bed_deposit: float32 [32, 512], P(('arch', 'dom'))
Inputs may be any that keep to these rules, and one draw needn't show every extreme that they name: `block_tile`: in every step each block's tile belongs to the group of the block's dom index d: (tile) % 16 equals d. Within each group, tiles held at lower arch indices are used by more blocks than those at higher ones.
All inputs are finite; a program needn't handle non-finite values.
Results may differ from a plain program's by a relative error of at most 0.0003.
Values may be sent and summed in bfloat16 or wider, within the bound.
A program may use at most 64 MiB of HBM per device.

v0:
```python
import math

import jax
import jax.numpy as jnp
from jax import lax
from jax.sharding import PartitionSpec as P

TILE_ARCH = 1
BEDC = 512


time_step = 0.5


def build_lookup(earlier, later):
    stacked = jnp.concatenate([earlier[0], later[0], earlier[1][None], later[1][None]], 0)
    tile_count = stacked.shape[1]
    return stacked.reshape(8, tile_count, stacked.shape[2] // 128, 128).transpose(1, 0, 2, 3)


def interpolate(lookup, local_tile, cells):
    nblocks = local_tile.shape[0]
    bundle = math.gcd(nblocks, 4)
    tile_count = lookup.shape[0]
    row_count = lookup.shape[2]
    lane_ids = jnp.arange(128, dtype=jnp.int32)
    row_ids = jnp.arange(row_count, dtype=jnp.int32)
    tile_ids = jnp.arange(tile_count, dtype=jnp.int32)

    def interpolate_one_bundle(pieces):
        tile_bundle, cell_bundle = pieces
        column_hit = ((cell_bundle % 128)[..., None] == lane_ids).astype(jnp.bfloat16)
        partial_value = jnp.einsum(
            "tqrc,gpc->gtqrp", lookup, column_hit, preferred_element_type=jnp.float32
        )
        row_hit = ((cell_bundle // 128)[:, None, :] == row_ids[None, :, None]).astype(jnp.float32)
        tile_hit = (tile_bundle[:, None] == tile_ids[None, :]).astype(jnp.float32)
        joint = tile_hit[:, :, None, None] * row_hit[:, None]
        return jnp.sum(partial_value * joint[:, :, None], axis=(1, 3))

    sampled = lax.map(
        interpolate_one_bundle,
        (
            local_tile.reshape(nblocks // bundle, bundle),
            cells.reshape(nblocks // bundle, bundle, -1),
        ),
    )
    return sampled.reshape(nblocks, 8, -1)


def deposit_bed(deposit, local_tile, bed_cells, tile_count):
    nblocks = local_tile.shape[0]
    bundle = math.gcd(nblocks, 8)
    tile_ids = jnp.arange(tile_count, dtype=jnp.int32)
    bed_ids = jnp.arange(BEDC, dtype=jnp.int32)

    def deposit_one_bundle(pieces):
        dep_bundle, tile_bundle, bed_bundle = pieces
        tile_hit = (tile_bundle[:, None] == tile_ids[None, :]).astype(jnp.float32)
        weighted = dep_bundle[:, None, :] * tile_hit[:, :, None]
        bed_hit = (bed_bundle[..., None] == bed_ids).astype(jnp.float32)
        return jnp.einsum("gtw,gwc->tc", weighted, bed_hit, precision=lax.Precision.HIGHEST)

    width = deposit.shape[1]
    pieces = (
        deposit.reshape(nblocks // bundle, bundle, width),
        local_tile.reshape(nblocks // bundle, bundle),
        bed_cells.reshape(nblocks // bundle, bundle, width),
    )
    return jnp.sum(lax.map(deposit_one_bundle, pieces), axis=0)


def permute_blocks(order, state):
    nblocks = order.shape[0]
    slot_ids = jnp.arange(nblocks, dtype=jnp.int32)
    mover = (order[None, :] == slot_ids[:, None]).astype(jnp.float32)
    flat = state.reshape(nblocks, -1)
    moved = jnp.dot(
        mover, flat, precision=lax.Precision.HIGHEST, preferred_element_type=jnp.float32
    )
    return moved.reshape(state.shape)


def body(
    position,
    particle_mass,
    settling,
    walk_noise,
    velocity,
    diffusivity,
    block_tile,
    cell_index,
    bed_cell,
    route_code,
):
    dom_count = lax.axis_size("dom")
    arch_count = lax.axis_size("arch")
    particles = position.shape[1]
    nblocks = block_tile.shape[2]
    width = particles // nblocks
    per_peer = nblocks // dom_count
    tiles_group = TILE_ARCH * arch_count
    slabs = velocity.shape[0]
    steps = cell_index.shape[0]
    places = position.reshape(3, nblocks, width).transpose(1, 0, 2)
    carried = jnp.stack([particle_mass, settling], 0).reshape(2, nblocks, width).transpose(1, 0, 2)
    whole_velocity, whole_diffusivity = (
        lax.all_gather(velocity, "arch", axis=2, tiled=True),
        lax.all_gather(diffusivity, "arch", axis=1, tiled=True),
    )
    archive = [(whole_velocity[slab], whole_diffusivity[slab]) for slab in range(slabs)]
    bed_share = jnp.zeros((TILE_ARCH, BEDC), jnp.float32)
    for step in range(steps):
        lookup = build_lookup(archive[step], archive[step + 1])
        global_tile = block_tile[step, 0]
        local_tile = global_tile // TILE_ARCH // dom_count * TILE_ARCH + global_tile % TILE_ARCH
        cells = cell_index[step].reshape(nblocks, width)
        sampled = interpolate(lookup, local_tile, cells)
        masses = carried[:, 0]
        speeds = carried[:, 1]
        drift = 0.5 * time_step * (sampled[:, 0:3] + sampled[:, 3:6])
        drift = drift.at[:, 2].add(-time_step * speeds)
        noise_now = walk_noise[step].reshape(3, nblocks, width).transpose(1, 0, 2)
        spread = jnp.sqrt(time_step * (sampled[:, 6] + sampled[:, 7]))
        places = places + drift + spread[:, None] * noise_now
        deposit = masses * (1.0 - jnp.exp(-time_step * speeds))
        masses = masses - deposit
        partial_value = deposit_bed(
            deposit, local_tile, bed_cell[step].reshape(nblocks, width), tiles_group
        )
        bed_share = bed_share + lax.psum_scatter(
            partial_value, "arch", scatter_dimension=0, tiled=True
        )
        carried = jnp.stack([masses, speeds], 1)
        if step + 1 < steps:
            order = route_code[step, 0]
            particle_state = jnp.concatenate([places, carried], 1)
            outgoing = permute_blocks(order, particle_state)
            incoming = lax.all_to_all(
                outgoing.reshape(dom_count, per_peer, 5, width),
                "dom",
                split_axis=0,
                concat_axis=0,
                tiled=True,
            )
            incoming = incoming.reshape(nblocks, 5, width)
            places = incoming[:, 0:3]
            carried = incoming[:, 3:5]
    final_places = places.transpose(1, 0, 2).reshape(3, particles)
    final_carried = carried.transpose(1, 0, 2).reshape(2, particles)
    scale_factor = TILE_ARCH * BEDC / particles
    return (final_places, final_carried[0], bed_share * scale_factor)


def solution(mesh):
    return jax.shard_map(
        body,
        mesh=mesh,
        in_specs=(
            P(None, ("arch", "dom")),
            P(("arch", "dom")),
            P(("arch", "dom")),
            P(None, None, ("arch", "dom")),
            P(None, None, ("arch", "dom"), None),
            P(None, ("arch", "dom"), None),
            P(None, ("arch", "dom"), None),
            P(None, ("arch", "dom")),
            P(None, ("arch", "dom")),
            P(None, ("arch", "dom"), None),
        ),
        out_specs=(P(None, ("arch", "dom")), P(("arch", "dom")), P(("arch", "dom"), None)),
        check_vma=False,
    )
```

profile of v0, /device:TPU:0, one launch (start us, length us, event | category | flops | bytes accessed | tf_op | source)
XLA Modules:
  0.0 54.6 jit_solution(8992151976181056654)
XLA Ops:
  0.6 0.7 %slice_reduce_fusion.11 = (s32[16]{0:T(128)S(1)}, s32[16]{0:T(128)S(1)}, s32[16]{0:T(128)S(1)}, s32[16]{0:T(128)S(1)}, s32[16]{0:T(128)S(1)}, /*index=5*/s32[16]{0:T(128)S(1)}) fusion(s32[3,1,16]{2,1,0:T(1,128)} %param.34), kind=kLoop, calls=%fused_computation.250 | loop fusion | bytes 576 | tf_op jit(solution)/shard_map/slice | solution.py:115
  1.5 2.2 %all_gather.7 = bf16[4,2,2048]{2,0,1:T(4,128)(2,1)S(1)} all-gather(bf16[4,1,2048]{2,0,1:T(4,128)(2,1)} %param.33), channel_id=1, replica_groups=mesh['arch'=2,'dom'=16] {'arch'}, dimensions={1}, use_global_device_ids=true | all-gather | bytes 49152 | tf_op jit(solution)/shard_map/all_gather | solution.py:109
  3.7 1.9 %all_gather.6 = bf16[4,3,2,2048]{3,0,2,1:T(4,128)(2,1)S(1)} all-gather(bf16[4,3,1,2048]{3,0,2,1:T(4,128)(2,1)S(1)} %copy-done.2), channel_id=1, replica_groups=mesh['arch'=2,'dom'=16] {'arch'}, dimensions={2}, use_global_device_ids=true | all-gather | bytes 147456 | tf_op jit(solution)/shard_map/all_gather | solution.py:108
  5.6 0.5 slice_reduce_fusion.3
  6.3 0.8 %copy-done.3 = s32[3,4096]{1,0:T(4,128)S(1)} copy-done((s32[3,4096]{1,0:T(4,128)S(1)}, s32[3,4096]{1,0:T(4,128)}, u32[]{:S(2)}) %copy-start.3) | copy-done | bytes 49176
  7.4 2.7 %while.75 = (s32[]{:T(128)}, f32[4,4,8,256]{3,2,1,0:T(8,128)S(1)}, s32[4,4,256]{2,1,0:T(4,128)S(1)}, bf16[2,8,16,128]{3,2,1,0:T(8,128)(2,1)S(1)}, s32[4,4]{1,0:T(4,128)S(1)}, /*index=5*/s32[]{:T(128)}) while((s32[]{:T(128)}, f32[4,4,8,256]{3,2,1,0:T(8,128)S(1)}, s32[4,4,256]{2,1,0:T(4,128)S(1)}, ...), condition=%wide.region_2.3_spmd.clone, body=%wide.region_0.2_spmd.clone.sunk | while | flops 67841040 | bytes 577737 | solution.py:41
  7.6 0.4 fusion.178
  8.3 0.4 fusion.178
  10.2 0.6 %copy-done.7 = s32[2,1,16]{2,1,0:T(1,128)S(1)} copy-done((s32[2,1,16]{2,1,0:T(1,128)S(1)}, s32[2,1,16]{2,1,0:T(1,128)}, u32[]{:S(2)}) %copy-start.7) | copy-done | bytes 152
  11.2 0.7 %copy-done.1 = f32[3,4096]{1,0:T(4,128)S(1)} copy-done((f32[3,4096]{1,0:T(4,128)S(1)}, f32[3,4096]{1,0:T(4,128)}, u32[]{:S(2)}) %copy-start.1) | copy-done | bytes 49176
  12.2 0.7 %copy.58 = f32[16,1,5,256]{3,1,2,0:T(1,128)} copy(f32[16,1,5,256]{3,0,2,1:T(8,128)S(1)} %convolution_bitcast_fusion.4) | data formatting | bytes 163840 | tf_op jit(solution)/shard_map/dot_general | solution.py:78
  12.9 8.2 %all-to-all-start = ((f32[16,1,5,256]{3,1,2,0:T(1,128)}), f32[16,1,5,256]{3,1,2,0:T(1,128)S(1)}, u32[]{:S(2)}, u32[]{:S(2)}) async-start(f32[16,1,5,256]{3,1,2,0:T(1,128)} %copy.58), calls=%async_computation | async-start | bytes 163840 | tf_op jit(solution)/shard_map/all_to_all | solution.py:139
  21.2 2.7 %while.76 = (s32[]{:T(128)}, f32[4,4,8,256]{3,2,1,0:T(8,128)S(1)}, s32[4,4,256]{2,1,0:T(4,128)S(1)}, bf16[2,8,16,128]{3,2,1,0:T(8,128)(2,1)S(1)}, s32[4,4]{1,0:T(4,128)S(1)}, /*index=5*/s32[]{:T(128)}) while((s32[]{:T(128)}, f32[4,4,8,256]{3,2,1,0:T(8,128)S(1)}, s32[4,4,256]{2,1,0:T(4,128)S(1)}, ...), condition=%wide.region_5.6_spmd.clone, body=%wide.region_3.5_spmd.clone.sunk | while | flops 67841040 | bytes 577737 | solution.py:41
  22.1 0.4 fusion.184
  24.1 2.7 %while.77 = (s32[]{:T(128)}, f32[4,4,8,256]{3,2,1,0:T(8,128)S(1)}, s32[4,4,256]{2,1,0:T(4,128)S(1)}, bf16[2,8,16,128]{3,2,1,0:T(8,128)(2,1)S(1)}, s32[4,4]{1,0:T(4,128)S(1)}, /*index=5*/s32[]{:T(128)}) while((s32[]{:T(128)}, f32[4,4,8,256]{3,2,1,0:T(8,128)S(1)}, s32[4,4,256]{2,1,0:T(4,128)S(1)}, ...), condition=%wide.region_8.9_spmd.clone, body=%wide.region_6.8_spmd.clone.sunk | while | flops 67841040 | bytes 577737 | solution.py:41
  27.2 3.1 %while.78 = (s32[]{:T(128)}, f32[2,2,512]{2,1,0:T(2,128)S(1)}, f32[2,8,256]{2,1,0:T(8,128)S(1)}, s32[2,8]{1,0:T(2,128)S(1)}, s32[2,8,256]{2,1,0:T(8,128)S(1)}, /*index=5*/s32[]{:T(128)}) while((s32[]{:T(128)}, f32[2,2,512]{2,1,0:T(2,128)S(1)}, f32[2,8,256]{2,1,0:T(8,128)S(1)}, s32[2,8]{1,0:T(2,128)S(1)}, ...), condition=%wide.region_10.11_spmd.clone, body=%wide.region_9.10_spmd.clone.sunk | while | flops 26218528 | bytes 57597 | solution.py:70
  27.3 1.4 %fusion.194 = f32[2,2,512]{2,1,0:T(2,128)S(1)} fusion(f32[2,2,512]{2,1,0:T(2,128)S(1)} %get-tuple-element.1008, s32[]{:T(128)S(6)} %copy.200, s32[8,256]{1,0:T(8,128)S(1)} %dynamic-slice_bitcast_fusion.12, f32[8,2]{1,0:T(8,128)S(1)} %fusion.193, f32[8,256]{1,0:T(8,128)S(1)} %dynamic-slice_bitcast_fusion.13), kind=kOutput, calls=%fused_computation.94.clone.1 | convolution fusion | flops 26218496 | bytes 24580 | tf_op jit(solution)/shard_map/while/body/eval_jaxpr/gtw,gwc->tc/dot_general | solution.py:62
  28.9 1.4 %fusion.194 = f32[2,2,512]{2,1,0:T(2,128)S(1)} fusion(f32[2,2,512]{2,1,0:T(2,128)S(1)} %get-tuple-element.1008, s32[]{:T(128)S(6)} %copy.200, s32[8,256]{1,0:T(8,128)S(1)} %dynamic-slice_bitcast_fusion.12, f32[8,2]{1,0:T(8,128)S(1)} %fusion.193, f32[8,256]{1,0:T(8,128)S(1)} %dynamic-slice_bitcast_fusion.13), kind=kOutput, calls=%fused_computation.94.clone.1 | convolution fusion | flops 26218496 | bytes 24580 | tf_op jit(solution)/shard_map/while/body/eval_jaxpr/gtw,gwc->tc/dot_general | solution.py:62
  30.3 0.6 %dynamic-slice.24 = u32[1]{0:T(128)} dynamic-slice(u32[32]{0:T(128)S(1)} %copy-done.8, u32[]{:T(128)S(6)} %add.228), dynamic_slice_sizes={1} | dynamic-slice | bytes 12
  31.3 0.7 %copy.65 = f32[16,1,5,256]{3,1,2,0:T(1,128)} copy(f32[16,1,5,256]{3,0,2,1:T(8,128)S(1)} %convolution_bitcast_fusion.3) | data formatting | bytes 163840 | tf_op jit(solution)/shard_map/dot_general | solution.py:78
  32.0 6.9 %all-to-all-start.1 = ((f32[16,1,5,256]{3,1,2,0:T(1,128)}), f32[16,1,5,256]{3,1,2,0:T(1,128)S(1)}, u32[]{:S(2)}, u32[]{:S(2)}) async-start(f32[16,1,5,256]{3,1,2,0:T(1,128)} %copy.65), calls=%async_computation.1 | async-start | bytes 163840 | tf_op jit(solution)/shard_map/all_to_all | solution.py:139
  38.9 3.1 %while.79 = (s32[]{:T(128)}, f32[2,2,512]{2,1,0:T(2,128)S(1)}, f32[2,8,256]{2,1,0:T(8,128)S(1)}, s32[2,8]{1,0:T(2,128)S(1)}, s32[2,8,256]{2,1,0:T(8,128)S(1)}, /*index=5*/s32[]{:T(128)}) while((s32[]{:T(128)}, f32[2,2,512]{2,1,0:T(2,128)S(1)}, f32[2,8,256]{2,1,0:T(8,128)S(1)}, s32[2,8]{1,0:T(2,128)S(1)}, ...), condition=%wide.region_14.15_spmd.clone, body=%wide.region_13.14_spmd.clone.sunk | while | flops 26218528 | bytes 57597 | solution.py:70
  39.0 1.4 %fusion.198 = f32[2,2,512]{2,1,0:T(2,128)S(1)} fusion(f32[2,2,512]{2,1,0:T(2,128)S(1)} %get-tuple-element.1026, s32[]{:T(128)S(6)} %copy.206, s32[8,256]{1,0:T(8,128)S(1)} %dynamic-slice_bitcast_fusion.14, f32[8,2]{1,0:T(8,128)S(1)} %fusion.197, f32[8,256]{1,0:T(8,128)S(1)} %dynamic-slice_bitcast_fusion.15), kind=kOutput, calls=%fused_computation.108.clone.1 | convolution fusion | flops 26218496 | bytes 24580 | tf_op jit(solution)/shard_map/while/body/eval_jaxpr/gtw,gwc->tc/dot_general | solution.py:62
  40.5 1.4 %fusion.198 = f32[2,2,512]{2,1,0:T(2,128)S(1)} fusion(f32[2,2,512]{2,1,0:T(2,128)S(1)} %get-tuple-element.1026, s32[]{:T(128)S(6)} %copy.206, s32[8,256]{1,0:T(8,128)S(1)} %dynamic-slice_bitcast_fusion.14, f32[8,2]{1,0:T(8,128)S(1)} %fusion.197, f32[8,256]{1,0:T(8,128)S(1)} %dynamic-slice_bitcast_fusion.15), kind=kOutput, calls=%fused_computation.108.clone.1 | convolution fusion | flops 26218496 | bytes 24580 | tf_op jit(solution)/shard_map/while/body/eval_jaxpr/gtw,gwc->tc/dot_general | solution.py:62
  42.0 4.5 %all-to-all-done.1 = f32[16,1,5,256]{3,1,2,0:T(1,128)S(1)} async-done(((f32[16,1,5,256]{3,1,2,0:T(1,128)}), f32[16,1,5,256]{3,1,2,0:T(1,128)S(1)}, u32[]{:S(2)}, u32[]{:S(2)}) %all-to-all-start.1) | async-done | bytes 81952 | tf_op jit(solution)/shard_map/all_to_all | solution.py:139
  46.5 3.1 %while.80 = (s32[]{:T(128)}, f32[2,2,512]{2,1,0:T(2,128)S(1)}, f32[2,8,256]{2,1,0:T(8,128)S(1)}, s32[2,8]{1,0:T(2,128)S(1)}, s32[2,8,256]{2,1,0:T(8,128)S(1)}, /*index=5*/s32[]{:T(128)}) while((s32[]{:T(128)}, f32[2,2,512]{2,1,0:T(2,128)S(1)}, f32[2,8,256]{2,1,0:T(8,128)S(1)}, s32[2,8]{1,0:T(2,128)S(1)}, ...), condition=%wide.region_18.19_spmd.clone, body=%wide.region_17.18_spmd.clone.sunk | while | flops 26218528 | bytes 57597 | solution.py:70
  46.6 1.4 %fusion.202 = f32[2,2,512]{2,1,0:T(2,128)S(1)} fusion(f32[2,2,512]{2,1,0:T(2,128)S(1)} %get-tuple-element.990, s32[]{:T(128)S(6)} %copy.194, s32[8,256]{1,0:T(8,128)S(1)} %dynamic-slice_bitcast_fusion.16, f32[8,2]{1,0:T(8,128)S(1)} %fusion.201, f32[8,256]{1,0:T(8,128)S(1)} %dynamic-slice_bitcast_fusion.17), kind=kOutput, calls=%fused_computation.122.clone.1 | convolution fusion | flops 26218496 | bytes 24580 | tf_op jit(solution)/shard_map/while/body/eval_jaxpr/gtw,gwc->tc/dot_general | solution.py:62
  48.2 1.4 %fusion.202 = f32[2,2,512]{2,1,0:T(2,128)S(1)} fusion(f32[2,2,512]{2,1,0:T(2,128)S(1)} %get-tuple-element.990, s32[]{:T(128)S(6)} %copy.194, s32[8,256]{1,0:T(8,128)S(1)} %dynamic-slice_bitcast_fusion.16, f32[8,2]{1,0:T(8,128)S(1)} %fusion.201, f32[8,256]{1,0:T(8,128)S(1)} %dynamic-slice_bitcast_fusion.17), kind=kOutput, calls=%fused_computation.122.clone.1 | convolution fusion | flops 26218496 | bytes 24580 | tf_op jit(solution)/shard_map/while/body/eval_jaxpr/gtw,gwc->tc/dot_general | solution.py:62
  49.7 2.5 %all-reduce = f32[2,512]{1,0:T(2,128)S(1)} all-reduce(f32[2,512]{1,0:T(2,128)S(1)} %add_add_fusion), channel_id=4, replica_groups=mesh['arch'=2,'dom'=16] {'arch'}, use_global_device_ids=true, to_apply=%region_12.13.clone | all-reduce | flops 1024 | bytes 8192
  52.2 0.7 %copy.99 = f32[1,3,16,256]{3,1,2,0:T(4,128)} copy(f32[1,3,16,256]{3,2,1,0:T(8,128)S(1)} %fusion.96) | data formatting | bytes 98304
  52.8 0.6 %copy.100 = f32[2,2,8,128]{3,1,2,0:T(2,128)} copy(f32[2,2,8,128]{3,2,1,0:T(8,128)S(1)} %slice_bitcast_fusion) | data formatting | bytes 32768
  53.4 1.1 %dynamic-slice_multiply_fusion = f32[1,512]{1,0:T(1,128)} fusion(f32[2,512]{1,0:T(2,128)S(1)} %all-reduce, u32[]{:T(128)} %bitcast.65), kind=kLoop, calls=%fused_computation.227 | loop fusion | flops 512 | bytes 4100 | tf_op jit(solution)/shard_map/mul | solution.py:152
  (190 shorter events, 8.9 us)
Async XLA Ops:
  0.6 3.1 %copy-start.2 = (bf16[4,3,1,2048]{3,0,2,1:T(4,128)(2,1)S(1)}, bf16[4,3,1,2048]{3,0,2,1:T(4,128)(2,1)}, u32[]{:S(2)}) copy-start(bf16[4,3,1,2048]{3,0,2,1:T(4,128)(2,1)} %param.32) | copy-start | bytes 147460
  6.2 0.8 %copy-start.3 = (s32[3,4096]{1,0:T(4,128)S(1)}, s32[3,4096]{1,0:T(4,128)}, u32[]{:S(2)}) copy-start(s32[3,4096]{1,0:T(4,128)} %param.36) | copy-start | bytes 147460
  6.2 0.9 %copy-start.4 = (s32[3,4096]{1,0:T(4,128)S(1)}, s32[3,4096]{1,0:T(4,128)}, u32[]{:S(2)}) copy-start(s32[3,4096]{1,0:T(4,128)} %param.35) | copy-start | bytes 147460
  10.1 0.7 %copy-start.7 = (s32[2,1,16]{2,1,0:T(1,128)S(1)}, s32[2,1,16]{2,1,0:T(1,128)}, u32[]{:S(2)}) copy-start(s32[2,1,16]{2,1,0:T(1,128)} %param.37) | copy-start | bytes 388
  10.1 0.7 %copy-start.5 = (f32[4096]{0:T(1024)S(1)}, f32[4096]{0:T(1024)}, u32[]{:S(2)}) copy-start(f32[4096]{0:T(1024)} %param.29) | copy-start | bytes 49156
  10.1 0.7 %copy-start.6 = (f32[4096]{0:T(1024)S(1)}, f32[4096]{0:T(1024)}, u32[]{:S(2)}) copy-start(f32[4096]{0:T(1024)} %param.30) | copy-start | bytes 49156
  10.1 0.9 %copy-start = (f32[3,3,4096]{2,1,0:T(4,128)S(1)}, f32[3,3,4096]{2,1,0:T(4,128)}, u32[]{:S(2)}) copy-start(f32[3,3,4096]{2,1,0:T(4,128)} %param.31) | copy-start | bytes 442372
  11.1 0.8 %copy-start.1 = (f32[3,4096]{1,0:T(4,128)S(1)}, f32[3,4096]{1,0:T(4,128)}, u32[]{:S(2)}) copy-start(f32[3,4096]{1,0:T(4,128)} %param.28) | copy-start | bytes 147460
  12.9 18.2 %all-to-all-start = ((f32[16,1,5,256]{3,1,2,0:T(1,128)}), f32[16,1,5,256]{3,1,2,0:T(1,128)S(1)}, u32[]{:S(2)}, u32[]{:S(2)}) async-start(f32[16,1,5,256]{3,1,2,0:T(1,128)} %copy.58), calls=%async_computation | async-start | bytes 163840 | tf_op jit(solution)/shard_map/all_to_all | solution.py:139
  27.2 3.1 %copy-start.8 = (u32[32]{0:T(128)S(1)}, u32[32]{0:T(128)}, u32[]{:S(2)}) copy-start(u32[32]{0:T(128)} %constant.383) | copy-start | bytes 388
  32.0 14.5 %all-to-all-start.1 = ((f32[16,1,5,256]{3,1,2,0:T(1,128)}), f32[16,1,5,256]{3,1,2,0:T(1,128)S(1)}, u32[]{:S(2)}, u32[]{:S(2)}) async-start(f32[16,1,5,256]{3,1,2,0:T(1,128)} %copy.65), calls=%async_computation.1 | async-start | bytes 163840 | tf_op jit(solution)/shard_map/all_to_all | solution.py:139
where the time goes:
time: 55.1 us; the launch traced here: 54.6 us
  starting transfers between devices  15.1 us (27%)
  matrix products  14.2 us (26%)
  local copies, waits for them, and re-layouts  8.44 us (15%)
  blocking collectives  6.5 us (12%)
  waiting for transfers between devices  4.49 us (8%)
  other arithmetic  3.94 us (7%)
  between operations  1.12 us (2%)
  loops' own time  0.75 us (1%)
    all_to_all x2, starting transfers between devices, body(): lax.all_to_all(outgoing.reshape(dom_count, per_peer, 5, width), 'dom', sp...  15.1 us
    dot_general x6, matrix products, deposit_one_bundle(): jnp.einsum('gtw,gwc->tc', weighted, bed_hit, precision=lax.Precision.HIGH...  8.66 us
    dot_general x12, matrix products, interpolate_one_bundle(): jnp.einsum('tqrc,gpc->gtqrp', lookup, column_hit, preferred_element_type=...  5.24 us
    all_to_all x2, waiting for transfers between devices, body(): lax.all_to_all(outgoing.reshape(dom_count, per_peer, 5, width), 'dom', sp...  4.49 us
    unnamed x25, local copies, waits for them, and re-layouts  4.33 us
    unnamed x1, blocking collectives  2.47 us
    all_gather x1, blocking collectives, body(): lax.all_gather(diffusivity, 'arch', axis=1, tiled=True)  2.15 us
    all_gather x1, blocking collectives, body(): lax.all_gather(velocity, 'arch', axis=2, tiled=True)  1.88 us
  transfers between devices with their start and end apart: 2, of which 1 were waited for; matrix products, arithmetic and copies ran while one was open for 23% of the time, Pallas kernels for 0%

commit v1 on v0

v1 whole, which is shorter than its diff:
```python
import functools
import math

import jax
import jax.numpy as jnp
from jax import lax
from jax.experimental import pallas as pl
from jax.experimental.pallas import tpu as pltpu
from jax.sharding import PartitionSpec as P

MESH = pl.DeviceIdType.MESH
BF16 = jnp.bfloat16
F32 = jnp.float32

BEDC = 512
LANES = 128
time_step = 0.5


def kernel(
    doms, archs, nblocks, width, steps, slabs, rows, scale,
    pos_hbm, mass_hbm, settle_hbm, noise_hbm, vel_hbm, diff_hbm, tile_hbm, cell_hbm, bed_hbm, route_hbm,
    pos_out, mass_out, bed_out,
    pos, mass, settle, noise, vel, diff, tile, cell, bed, route,
    spread_rows, table, inverse, decay, dep, delta,
    carried_send, carried_recv, pos_send, pos_recv,
    bed_part, bed_recv,
    in_sem, table_sem, carried_sem, pos_sem, bed_sem,
):
    me = lax.axis_index("dom")
    arch = lax.axis_index("arch")
    twin = lax.rem(arch + 1, archs)
    group = math.gcd(nblocks, 8)

    barrier = pltpu.get_barrier_semaphore()

    def greet(p, _):
        pl.semaphore_signal(barrier, inc=1, device_id={"dom": lax.rem(me + p, doms)}, device_id_type=MESH)
        return 0

    lax.fori_loop(1, doms, greet, 0)
    pl.semaphore_signal(barrier, inc=1, device_id={"arch": twin}, device_id_type=MESH)

    staged = [
        pltpu.make_async_copy(src, dst, in_sem.at[i])
        for i, (src, dst) in enumerate(
            [
                (tile_hbm, tile), (route_hbm, route), (vel_hbm, vel), (diff_hbm, diff), (mass_hbm, mass),
                (settle_hbm, settle), (bed_hbm, bed), (cell_hbm, cell), (pos_hbm, pos), (noise_hbm, noise),
            ]
        )
    ]
    for copy in staged:
        copy.start()
    for copy in staged[:2]:
        copy.wait()

    for step in range(steps - 1):
        def invert(c, _, step=step):
            def probe(j, found):
                return jnp.where(route[step, 0, j] == c, j, found)

            inverse[step, c] = lax.fori_loop(0, nblocks, probe, jnp.int32(0), unroll=True if nblocks <= 16 else 16)
            return 0

        lax.fori_loop(0, nblocks, invert, 0)

    for copy in staged[2:4]:
        copy.wait()
    for ch in range(4):
        raw = (vel[ch] if ch < 3 else diff[...]).astype(F32)
        for r in range(rows):
            spread_rows[ch, pl.ds(r, slabs, stride=rows), :] = raw[:, r * LANES : (r + 1) * LANES]
    for slab in range(slabs):
        for ch in range(4):
            table[arch, slab, ch] = spread_rows[ch, slab * rows : (slab + 1) * rows, :].astype(BF16)

    for copy in staged[4:7]:
        copy.wait()
    fade = jnp.exp(-time_step * settle[...])
    decay[...] = fade
    dep[...] = mass[...] * (1.0 - fade)
    mass[...] = mass[...] * fade

    pl.semaphore_wait(barrier, doms - 1 + archs - 1)

    table_copy = pltpu.make_async_remote_copy(
        src_ref=table.at[arch], dst_ref=table.at[arch], send_sem=table_sem.at[0], recv_sem=table_sem.at[1],
        device_id={"arch": twin}, device_id_type=MESH,
    )
    table_copy.start()

    def send(step, sbuf, rbuf, sem, p):
        pltpu.make_async_remote_copy(
            src_ref=sbuf[step].at[p], dst_ref=rbuf[step].at[me], send_sem=sem.at[step, 0], recv_sem=sem.at[step, 1],
            device_id={"dom": lax.rem(me + p, doms)}, device_id_type=MESH,
        ).start()

    def whole(step, sbuf, rbuf, sem):
        return pltpu.make_async_remote_copy(
            src_ref=sbuf[step].at[pl.ds(1, doms - 1)], dst_ref=rbuf[step].at[pl.ds(1, doms - 1)],
            send_sem=sem.at[step, 0], recv_sem=sem.at[step, 1],
            device_id={"dom": lax.rem(me + 1, doms)}, device_id_type=MESH,
        )

    def send_carried(step, source):
        def load(p):
            return source(inverse[step, lax.rem(me + p, doms)])

        m, e = load(0)
        carried_recv[step][me, 0:2, :] = m
        carried_recv[step][me, 2:4, :] = e

        def one(p, _):
            m, e = load(p)
            carried_send[step][p, 0:2, :] = m
            carried_send[step][p, 2:4, :] = e
            send(step, carried_send, carried_recv, carried_sem, p)
            return 0

        lax.fori_loop(1, doms, one, 0, unroll=5 if doms == 16 else 1)

    send_carried(0, lambda j: (mass[j], decay[j]))

    def deposits(step, total):
        bed_ids = lax.broadcasted_iota(jnp.int32, (LANES, width), 0)
        row_ids = lax.broadcasted_iota(jnp.int32, (8, width), 0)

        def several(k, total):
            weights, hits = [], []
            for i in range(group):
                j = k * group + i
                cells = bed[step : step + 1, pl.ds(pl.multiple_of(j * width, width), width)]
                local = lax.div(tile[step, 0, j], doms)
                home = local * (BEDC // LANES) + cells // LANES
                amount = jnp.concatenate([dep[j, 0:1, :], dep[j, 1:2, :]], axis=1)
                weight = jnp.where(home == row_ids, amount, 0.0)
                high = weight.astype(BF16)
                low = (weight - high.astype(F32)).astype(BF16)
                weights.append(jnp.concatenate([high, low], axis=0))
                hits.append(jnp.where(cells % LANES == bed_ids, 1.0, 0.0).astype(BF16))
            return total + lax.dot_general(
                jnp.concatenate(weights, axis=1), jnp.concatenate(hits, axis=1),
                (((1,), (1,)), ((), ())), preferred_element_type=F32,
            )

        return lax.fori_loop(0, nblocks // group, several, total)

    channel_ids = lax.broadcasted_iota(jnp.int32, (16, 2 * 4 * rows), 1) // rows % 4
    out_ids = lax.broadcasted_iota(jnp.int32, (16, 2 * 4 * rows), 0)
    mix = jnp.where(
        out_ids < 8,
        jnp.where(channel_ids == out_ids, 0.5 * time_step, 0.0),
        jnp.where(channel_ids == 3, time_step, 0.0),
    ).astype(BF16)
    lane_ids = lax.broadcasted_iota(jnp.int32, (LANES, width), 0)
    cell_rows = lax.broadcasted_iota(jnp.int32, (rows, width), 0)

    def walk(step, blocks):
        picked = []
        for j in blocks:
            cells = cell[step : step + 1, pl.ds(pl.multiple_of(j * width, width), width)]
            column_hit = jnp.where(cells % LANES == lane_ids, 1.0, 0.0).astype(BF16)
            row_hit = jnp.where(cells // LANES == cell_rows, 1.0, 0.0).astype(BF16)
            local = lax.div(tile[step, 0, j], doms)
            both = jnp.concatenate(
                [table[local, slab].reshape(4 * rows, LANES) for slab in (step, step + 1)], axis=0
            )
            found = jnp.dot(both, column_hit, preferred_element_type=F32).astype(BF16)
            found = found.reshape(8, rows, width) * row_hit[None]
            picked.append(found.reshape(8 * rows, width))
        mixed = jnp.dot(mix, jnp.concatenate(picked, axis=1), preferred_element_type=F32)
        moves = []
        for i, j in enumerate(blocks):
            part = mixed[:, i * width : (i + 1) * width]
            draw = noise[step, :, pl.ds(pl.multiple_of(j * width, width), width)]
            moves.append(part[0:3] + jnp.sqrt(part[8:11]) * draw)
        return moves

    third = (lax.broadcasted_iota(jnp.int32, (3, width), 0) == 2)

    for copy in staged[7:]:
        copy.wait()
    table_copy.wait_recv()

    def first(k, _):
        blocks = [k * group + i for i in range(group)]
        moves = walk(0, blocks)
        values = []
        for j, move in zip(blocks, moves):
            speed = jnp.concatenate([settle[j, 0:1, :], settle[j, 1:2, :]], axis=1)
            sink = jnp.where(third, steps * time_step * speed, 0.0)
            here = pos[:, pl.ds(pl.multiple_of(j * width, width), width)]
            values.append(here - sink + move)
        for j, value in zip(blocks, values):
            delta[j] = value
        return 0

    lax.fori_loop(0, nblocks // group, first, 0)

    def send_places(step, source):
        def one(p, _):
            pos_send[step][p] = source(inverse[step, lax.rem(me + p, doms)])
            send(step, pos_send, pos_recv, pos_sem, p)
            return 0

        lax.fori_loop(1, doms, one, 0, unroll=5 if doms == 16 else 1)
        pos_recv[step][me] = source(inverse[step, me])

    send_places(0, lambda j: delta[j])

    total = deposits(0, jnp.zeros((16, LANES), F32))

    def rest(step):
        def some(k, _):
            moves = walk(step, [k * group + i for i in range(group)])
            for i, move in enumerate(moves):
                delta[k * group + i] = move
            return 0

        lax.fori_loop(0, nblocks // group, some, 0)

    for step in range(1, steps):
        whole(step - 1, carried_send, carried_recv, carried_sem).wait_recv()
        masses = carried_recv[step - 1][:, 0:2, :]
        fade = carried_recv[step - 1][:, 2:4, :]
        left = masses * fade
        dep[...] = masses - left
        if step + 1 < steps:
            def source(j, step=step):
                fade = carried_recv[step - 1][j, 2:4, :]
                return carried_recv[step - 1][j, 0:2, :] * fade, fade

            send_carried(step, source)
        else:
            mass_out[...] = left
        rest(step)
        if step + 1 == steps:
            total = deposits(step, total)
            for t in range(archs):
                q = BEDC // LANES
                bed_part[t] = (total[t * q : (t + 1) * q] + total[8 + t * q : 8 + (t + 1) * q]) * scale
            bed_copy = pltpu.make_async_remote_copy(
                src_ref=bed_part.at[twin], dst_ref=bed_recv, send_sem=bed_sem.at[0], recv_sem=bed_sem.at[1],
                device_id={"arch": twin}, device_id_type=MESH,
            )
            bed_copy.start()
        whole(step - 1, pos_send, pos_recv, pos_sem).wait_recv()
        if step + 1 < steps:
            send_places(step, lambda j, step=step: pos_recv[step - 1][j] + delta[j])
            total = deposits(step, total)

    last = steps - 2
    def finish(j, _):
        pos_out[:, pl.ds(pl.multiple_of(j * width, width), width)] = pos_recv[last][j] + delta[j]
        return 0

    lax.fori_loop(0, nblocks, finish, 0, unroll=16)
    bed_copy.wait_recv()
    bed_out[...] = bed_part[arch] + bed_recv[...]

    table_copy.wait_send()
    bed_copy.wait_send()
    for step in range(steps - 1):
        whole(step, carried_send, carried_recv, carried_sem).wait_send()
        whole(step, pos_send, pos_recv, pos_sem).wait_send()


def body(
    position, particle_mass, settling, walk_noise, velocity, diffusivity, block_tile, cell_index, bed_cell, route_code
):
    doms = lax.axis_size("dom")
    archs = lax.axis_size("arch")
    particles = position.shape[1]
    nblocks = block_tile.shape[2]
    width = particles // nblocks
    steps = cell_index.shape[0]
    slabs, _, _, cells = velocity.shape
    rows = cells // LANES
    half = width // LANES
    moves = steps - 1
    in_hbm = pl.BlockSpec(memory_space=pltpu.HBM)
    in_vmem = pl.BlockSpec(memory_space=pltpu.VMEM)
    vmem = pltpu.VMEM
    args = (
        position,
        particle_mass.reshape(nblocks, half, LANES),
        settling.reshape(nblocks, half, LANES),
        walk_noise,
        velocity.transpose(1, 2, 0, 3).reshape(3, slabs, cells),
        diffusivity.transpose(1, 0, 2).reshape(slabs, cells),
        block_tile,
        cell_index,
        bed_cell,
        route_code,
    )
    places, masses, beds = pl.pallas_call(
        functools.partial(
            kernel, doms, archs, nblocks, width, steps, slabs, rows, BEDC / particles
        ),
        out_shape=(
            jax.ShapeDtypeStruct((3, particles), F32),
            jax.ShapeDtypeStruct((nblocks, half, LANES), F32),
            jax.ShapeDtypeStruct((BEDC // LANES, LANES), F32),
        ),
        in_specs=[in_hbm] * len(args),
        out_specs=(in_vmem, in_vmem, in_vmem),
        scratch_shapes=[
            vmem(args[0].shape, F32),
            vmem(args[1].shape, F32),
            vmem(args[2].shape, F32),
            vmem(args[3].shape, F32),
            vmem(args[4].shape, BF16),
            vmem(args[5].shape, BF16),
            pltpu.SMEM(args[6].shape, jnp.int32),
            vmem(args[7].shape, jnp.int32),
            vmem(args[8].shape, jnp.int32),
            pltpu.SMEM(args[9].shape, jnp.int32),
            vmem((4, slabs * rows, LANES), F32),
            vmem((archs, slabs, 4, rows, LANES), BF16),
            pltpu.SMEM((moves, nblocks), jnp.int32),
            vmem((nblocks, half, LANES), F32),
            vmem((nblocks, half, LANES), F32),
            vmem((nblocks, 3, width), F32),
            [vmem((nblocks, 2 * half, LANES), F32)] * moves,
            [vmem((nblocks, 2 * half, LANES), F32)] * moves,
            [vmem((nblocks, 3, width), F32)] * moves,
            [vmem((nblocks, 3, width), F32)] * moves,
            vmem((archs, BEDC // LANES, LANES), F32),
            vmem((BEDC // LANES, LANES), F32),
            pltpu.SemaphoreType.DMA((len(args),)),
            pltpu.SemaphoreType.DMA((2,)),
            pltpu.SemaphoreType.DMA((moves, 2)),
            pltpu.SemaphoreType.DMA((moves, 2)),
            pltpu.SemaphoreType.DMA((2,)),
        ],
        compiler_params=pltpu.CompilerParams(
            collective_id=0, has_side_effects=True, vmem_limit_bytes=60 * 1024 * 1024
        ),
    )(*args)
    return places, masses.reshape(particles), beds.reshape(1, BEDC)


def solution(mesh):
    return jax.shard_map(
        body,
        mesh=mesh,
        in_specs=(
            P(None, ("arch", "dom")),
            P(("arch", "dom")),
            P(("arch", "dom")),
            P(None, None, ("arch", "dom")),
            P(None, None, ("arch", "dom"), None),
            P(None, ("arch", "dom"), None),
            P(None, ("arch", "dom"), None),
            P(None, ("arch", "dom")),
            P(None, ("arch", "dom")),
            P(None, ("arch", "dom"), None),
        ),
        out_specs=(P(None, ("arch", "dom")), P(("arch", "dom")), P(("arch", "dom"), None)),
        check_vma=False,
    )
```

time: 55.1 us -> 22.6 us (0.41)
  Pallas kernels: 0 us -> 19 us
  starting transfers between devices: 15.1 us -> 0 us
  matrix products: 14.2 us -> 0 us
  blocking collectives: 6.5 us -> 0 us
  local copies, waits for them, and re-layouts: 8.44 us -> 2.74 us
  waiting for transfers between devices: 4.49 us -> 0 us
  other arithmetic: 3.94 us -> 0 us
  loops' own time: 0.75 us -> 0 us
    pallas_call x0 -> x1, Pallas kernels: none -> 19 us  [body(): pl.pallas_call(functools.partial(kernel, doms, archs, nblocks, width, ste...]
    all_to_all x2 -> x0, starting transfers between devices: 15.1 us -> none  [body(): lax.all_to_all(outgoing.reshape(dom_count, per_peer, 5, width), 'dom', sp...]
    dot_general x20 -> x0, matrix products: 14.2 us -> none  [the longest x6 8.66 us: deposit_one_bundle(): jnp.einsum('gtw,gwc->tc', weighted, bed_hit, precision=lax.Precision.HIGH...]
    all_to_all x2 -> x0, waiting for transfers between devices: 4.49 us -> none  [body(): lax.all_to_all(outgoing.reshape(dom_count, per_peer, 5, width), 'dom', sp...]
    all_gather x2 -> x0, blocking collectives: 4.03 us -> none  [the longest x1 2.15 us: body(): lax.all_gather(diffusivity, 'arch', axis=1, tiled=True)]
    unnamed x1 -> x0, blocking collectives: 2.47 us -> none
    mul x22 -> x0, other arithmetic: 2.21 us -> none  [the longest x1 1.14 us: body(): return (final_places, final_carried[0], bed_share * scale_factor)]
    slice x11 -> x0, local copies, waits for them, and re-layouts: 1.68 us -> none  [the longest x1 0.72 us: body(): global_tile = block_tile[step, 0]]
  transfers between devices with their start and end apart: 2 -> 0, of which waited for: 1 -> 0; matrix products, arithmetic and copies ran while one was open for 23% -> 0% of each run, Pallas kernels for 0% -> 0%
where the time goes in v1:
time: 22.6 us; the launch traced here: 22.4 us
  Pallas kernels  19 us (84%)
  local copies, waits for them, and re-layouts  2.74 us (12%)
  between operations  0.65 us (3%)
    pallas_call x1, Pallas kernels, body(): pl.pallas_call(functools.partial(kernel, doms, archs, nblocks, width, ste...  19 us
    unnamed x7, local copies, waits for them, and re-layouts  2.74 us

profile of v1, /device:TPU:0, one launch (start us, length us, event | category | flops | bytes accessed | tf_op | source)
XLA Modules:
  0.0 22.4 jit_solution(6352060576887402250)
XLA Ops:
  0.6 19.0 %shard_map.121 = (f32[3,4096]{1,0:T(4,128)}, f32[16,2,128]{2,1,0:T(2,128)}, f32[4,128]{1,0:T(4,128)}) custom-call(f32[3,4096]{1,0:T(4,128)} %pos_hbm.1, f32[16,2,128]{2,1,0:T(2,128)} %bitcast.11, f32[16,2,128]{2,1,0:T(2,128)} %bitcast.12, f32[3,3,4096]{2,1,0:T(4,128)} %noise_hbm.1, bf16[3,4,2048]{2,1,0:T(4,128)(2,1)} %bitcast.10, bf16[4,2048]{1,0:T(4,128)(2,1)} %bitcast.13, ...), custom_call_target="tpu_custom_call" | custom-call | tf_op jit(solution)/shard_map/pallas_call | solution.py:297
  19.7 0.0 copy-start
  19.7 1.5 %copy.17 = f32[3,4096]{1,0:T(4,128)} copy(f32[3,4096]{1,0:T(4,128)} %get-tuple-element.12) | data formatting | bytes 98304
  21.2 0.0 copy-done
  21.2 0.0 copy-start.1
  21.2 0.6 %copy.18 = f32[4096]{0:T(1024)} copy(f32[4096]{0:T(1024)S(1)} %bitcast.14) | data formatting | bytes 32768
  21.8 0.1 copy-done.1
  21.8 0.6 %copy.19 = f32[1,512]{1,0:T(1,128)} copy(f32[1,512]{1,0:T(1,128)S(1)} %bitcast.15) | data formatting | bytes 4096
Async XLA Ops:
  19.7 1.5 %copy-start = (f32[16,2,128]{2,1,0:T(2,128)S(1)}, f32[16,2,128]{2,1,0:T(2,128)}, u32[]{:S(2)}) copy-start(f32[16,2,128]{2,1,0:T(2,128)} %get-tuple-element.7) | copy-start | bytes 49156
  21.2 0.7 %copy-start.1 = (f32[4,128]{1,0:T(4,128)S(1)}, f32[4,128]{1,0:T(4,128)}, u32[]{:S(2)}) copy-start(f32[4,128]{1,0:T(4,128)} %get-tuple-element.8) | copy-start | bytes 6148
